TPU v7x, 256 devices: a whole 4x4x8 slice. The times are simulated.
256 devices in a mesh: section: 8 (over z), feat: 32 (over x, y, core).
Axes of the slice: x: 4, y: 4, z: 8, core: 2. Of those that a mesh axis runs over, the one named last changes fastest.
Arguments:
- inputs: bfloat16 [8, 512, 2560], P('section', 'feat'), may hold values from -6 to 6
- enc_weight: bfloat16 [8, 2560, 4096], P('section', None, 'feat'), may hold values from -0.125 to 0.125
- enc_bias: float32 [8, 4096], P('section', 'feat'), may hold values from -3 to 3
- dec_weight: bfloat16 [8, 8, 4096, 2560], P('section', None, 'feat'), may hold values from -0.09375 to 0.09375
- dec_bias: bfloat16 [8, 2560], P('section'), may hold values from -3 to 3
- target: bfloat16 [8, 512, 2560], P('section', 'feat'), may hold values from -6 to 6
- active: int32 [8, 16, 8], P('section'), may hold values from 0 to 31, all different within a row
Outputs:
- enc_grad: bfloat16 [8, 2560, 4096], P('section', None, 'feat')
- bias_grad: float32 [8, 4096], P('section', 'feat')
- dec_grad: bfloat16 [8, 8, 4096, 2560], P('section', None, 'feat')
Inputs may be any that keep to these rules, and one draw needn't show every extreme that they name: `active`: each row names 8 different blocks of 32; every block is named by some row.
All inputs are finite; a program needn't handle non-finite values.
Results may differ from a plain program's by a relative error of at most 0.024.
Values may be sent and summed in bfloat16 or wider, within the bound.
A program may use at most 128 MiB of HBM per device.

v0:
```python
import jax
import jax.numpy as jnp
from jax import lax
from jax.sharding import PartitionSpec as P

FBLK = 128


def block_mask(active_rows, first_feature, feat_width, tokens):
    feature_ids = first_feature + lax.iota(jnp.int32, feat_width)
    block_ids = feature_ids // FBLK
    matched = jnp.any(active_rows[:, :, None] == block_ids[None, None, :], axis=1)
    block_rows = tokens // active_rows.shape[0]
    return jnp.repeat(matched.astype(jnp.float32), block_rows, axis=0)


def body(inputs, enc_weight, enc_bias, dec_weight, dec_bias, target, active):
    section_index = lax.axis_index("section")
    feat_index = lax.axis_index("feat")
    feat_width = enc_weight.shape[2]
    layers = dec_weight.shape[1]
    whole_inputs = lax.all_gather(inputs[0], "feat", axis=0, tiled=True)
    tokens = whole_inputs.shape[0]
    keep_mask = block_mask(active[0], feat_index * feat_width, feat_width, tokens)
    pre_act = (
        jnp.dot(whole_inputs, enc_weight[0], preferred_element_type=jnp.float32)
        + enc_bias[0][None, :]
    )
    live_mask = keep_mask * (pre_act > 0).astype(jnp.float32)
    code_vals = (live_mask * pre_act).astype(jnp.bfloat16)
    layer_ids = lax.iota(jnp.int32, layers)
    causal = (layer_ids <= section_index).astype(jnp.bfloat16)
    visible = lax.all_gather(code_vals[None], "section", axis=0, tiled=True)
    visible = visible * causal[:, None, None]
    local_dec = dec_weight[0]
    bias_row = dec_bias[0].astype(jnp.float32)[None, :]
    code_rows = visible
    rebuilt = lax.psum_scatter(
        jnp.einsum("ltf,lfd->td", code_rows, local_dec, preferred_element_type=jnp.float32),
        "feat",
        scatter_dimension=0,
        tiled=True,
    )
    residual_part = (rebuilt + bias_row - target[0].astype(jnp.float32)).astype(jnp.bfloat16)
    rows_in = lax.all_gather(residual_part, "feat", axis=0, tiled=True)
    code_rows = visible
    grad_acc = jnp.einsum("ltf,td->lfd", code_rows, rows_in, preferred_element_type=jnp.float32)
    grad_block = jnp.einsum("td,lfd->ltf", rows_in, local_dec, preferred_element_type=jnp.float32)
    code_grad = grad_block
    grad_acc, code_grad = (grad_acc, code_grad)
    code_grad = code_grad * causal.astype(jnp.float32)[:, None, None]
    own_grad = lax.psum_scatter(code_grad, "section", scatter_dimension=0, tiled=True)[0]
    pre_grad = (own_grad * live_mask).astype(jnp.bfloat16)
    enc_grad = jnp.einsum(
        "td,tf->df", whole_inputs, pre_grad, preferred_element_type=jnp.float32
    ).astype(jnp.bfloat16)
    bias_grad = jnp.sum(pre_grad.astype(jnp.float32), axis=0)
    dec_grad = grad_acc.astype(jnp.bfloat16)
    return (enc_grad[None], bias_grad[None], dec_grad[None])


def solution(mesh):
    return jax.shard_map(
        body,
        mesh=mesh,
        in_specs=(
            P("section", "feat", None),
            P("section", None, "feat"),
            P("section", "feat"),
            P("section", None, "feat", None),
            P("section", None),
            P("section", "feat", None),
            P("section", None, None),
        ),
        out_specs=(
            P("section", None, "feat"),
            P("section", "feat"),
            P("section", None, "feat", None),
        ),
        check_vma=False,
    )
```

profile of v0, /device:TPU:1, one launch (start us, length us, event | category | flops | bytes accessed | tf_op | source)
XLA Modules:
  0.0 313.6 jit_solution(12986852656555350801)
XLA Ops:
  7.2 0.0 copy-start
  7.2 0.0 all-gather.8.cloned.1.call-start
  7.2 0.7 all-gather.8.cloned.1.call-update
  7.9 0.0 all-gather.10.cloned.1.call-start
  8.0 0.8 copy.14
  8.7 0.1 compare_reduce_fusion
  8.8 55.5 %all-gather.8.cloned.1.call-done = bf16[1,512,2560]{2,1,0:T(8,128)(2,1)} async-done(((bf16[1,16,2560]{2,1,0:T(8,128)(2,1)}), bf16[1,512,2560]{2,1,0:T(8,128)(2,1)}) %all-gather.8.cloned.1.call-update) | async-done | bytes 2621456 | tf_op jit(solution)/shard_map/all_gather | solution.py:22
  64.3 0.0 copy-done
  64.3 3.3 %fusion.28 = (bf16[512,128]{1,0:T(8,128)(2,1)}, f32[512,128]{1,0:T(8,128)S(1)}) fusion(f32[16,128]{1,0:T(8,128)S(1)} %convert_element_type.50, f32[128]{0:T(128)} %bitcast.65, bf16[1,2560,128]{2,1,0:T(8,128)(2,1)S(1)} %copy-done, bf16[1,512,2560]{2,1,0:T(8,128)(2,1)} %all-gather.8.cloned.1.call-done), kind=kOutput, calls=%fused_computation.25 | convolution fusion | flops 335872000 | bytes 3678720 | tf_op jit(solution)/shard_map/dot_general | solution.py:26
  67.6 0.0 all-gather.10.cloned.1.call-update
  67.6 0.0 reduce-scatter.3.cloned.1.call-start
  67.7 32.7 %all-gather.10.cloned.1.call-done = bf16[4096,128]{1,0:T(8,128)(2,1)} async-done(((bf16[512,128]{1,0:T(8,128)(2,1)}), bf16[4096,128]{1,0:T(8,128)(2,1)}) %all-gather.10.cloned.1.call-update) | async-done | bytes 1048592 | tf_op jit(solution)/shard_map/all_gather | solution.py:33
  100.4 1.5 copy.15
  101.9 0.0 copy-start.2
  101.9 7.6 %fusion.5 = f32[512,2560]{1,0:T(8,128)} fusion(bf16[1,8,128,2560]{3,2,1,0:T(8,128)(2,1)} %param.10, bf16[8,512,128]{1,2,0:T(8,128)(2,1)S(1)} %copy.15, bf16[8]{0:T(256)(128)(2,1)S(1)} %compare_convert_fusion), kind=kOutput, calls=%fused_computation.6 | convolution fusion | flops 2684878848 | bytes 11534352 | tf_op jit(solution)/shard_map/ltf,lfd->td/dot_general | solution.py:39
  109.5 0.0 copy-done.2
  109.5 0.0 copy-start.4
  109.5 0.0 copy-start.3
  109.5 0.0 reduce-scatter.3.cloned.1.call-update
  109.5 0.0 all-gather.6.cloned.1.call-start
  109.6 0.6 copy-done.4
  110.2 93.6 %reduce-scatter.3.cloned.1.call-done = f32[16,2560]{1,0:T(8,128)} async-done(((f32[512,2560]{1,0:T(8,128)}), f32[16,2560]{1,0:T(8,128)}) %reduce-scatter.3.cloned.1.call-update) | async-done | bytes 163856 | tf_op jit(solution)/shard_map/reduce_scatter | solution.py:38
  203.9 0.0 copy-done.3
  203.9 1.6 fusion.29
  205.4 0.0 all-gather.6.cloned.1.call-update
  205.5 0.0 reduce-scatter.5.cloned.1.call-start
  205.5 52.7 %all-gather.6.cloned.1.call-done = bf16[512,2560]{1,0:T(8,128)(2,1)} async-done(((bf16[16,2560]{1,0:T(8,128)(2,1)}), bf16[512,2560]{1,0:T(8,128)(2,1)}) %all-gather.6.cloned.1.call-update) | async-done | bytes 2621456 | tf_op jit(solution)/shard_map/all_gather | solution.py:45
  258.2 6.6 %multiply_bitcast_fusion = f32[8,512,128]{2,1,0:T(8,128)} fusion(bf16[1,8,128,2560]{3,2,1,0:T(8,128)(2,1)} %param.10, bf16[512,2560]{1,0:T(8,128)(2,1)} %all-gather.6.cloned.1.call-done, f32[8]{0:T(128)S(1)} %fusion.30), kind=kOutput, calls=%fused_computation.14 | convolution fusion | flops 2684878848 | bytes 9961504 | tf_op jit(solution)/shard_map/td,lfd->ltf/dot_general | solution.py:48
  264.8 0.0 reduce-scatter.5.cloned.1.call-update
  264.8 0.0 copy-start.1
  264.9 7.5 %fusion.4 = bf16[1,8,128,2560]{3,2,1,0:T(8,128)(2,1)} fusion(bf16[512,2560]{1,0:T(8,128)(2,1)} %all-gather.6.cloned.1.call-done, bf16[8,512,128]{1,2,0:T(8,128)(2,1)} %copy-done.2, bf16[8]{0:T(256)(128)(2,1)S(1)} %compare_convert_fusion), kind=kOutput, calls=%fused_computation.5 | convolution fusion | flops 2687500288 | bytes 8912912 | tf_op jit(solution)/shard_map/ltf,td->lfd/dot_general | solution.py:47
  272.3 29.7 %reduce-scatter.5.cloned.1.call-done = f32[1,512,128]{2,1,0:T(8,128)} async-done(((f32[8,512,128]{2,1,0:T(8,128)}), f32[1,512,128]{2,1,0:T(8,128)}) %reduce-scatter.5.cloned.1.call-update) | async-done | bytes 262160 | tf_op jit(solution)/shard_map/reduce_scatter | solution.py:52
  302.0 1.5 convert_reduce_fusion
  303.6 0.0 copy-done.1
  303.6 1.4 fusion.8
  305.0 2.2 copy.17
  (5 shorter events, 0.1 us)
Async XLA Ops:
  7.2 57.1 %copy-start = (bf16[1,2560,128]{2,1,0:T(8,128)(2,1)S(1)}, bf16[1,2560,128]{2,1,0:T(8,128)(2,1)}, u32[]{:S(2)}) copy-start(bf16[1,2560,128]{2,1,0:T(8,128)(2,1)} %param.8) | copy-start | bytes 1966084
  7.2 57.1 %all-gather.8.cloned.1.call-start = ((), (), s32[]{:S(2)}) async-start(), calls=%async_computation.5 | async-start | bytes 2703360 | tf_op jit(solution)/shard_map/all_gather | solution.py:22
  7.9 92.5 %all-gather.10.cloned.1.call-start = ((), (), s32[]{:S(2)}) async-start(), calls=%async_computation.6 | async-start | bytes 1179648 | tf_op jit(solution)/shard_map/all_gather | solution.py:33
  67.6 136.3 %reduce-scatter.3.cloned.1.call-start = ((), (), s32[]{:S(2)}) async-start(), calls=%async_computation.2 | async-start | bytes 5406720 | tf_op jit(solution)/shard_map/reduce_scatter | solution.py:38
  101.9 7.6 %copy-start.2 = (bf16[8,512,128]{1,2,0:T(8,128)(2,1)}, bf16[8,512,128]{1,2,0:T(8,128)(2,1)S(1)}, u32[]{:S(2)}) copy-start(bf16[8,512,128]{1,2,0:T(8,128)(2,1)S(1)} %copy.15) | copy-start | bytes 3145732
  109.5 0.7 copy-start.4
  109.5 94.4 %copy-start.3 = (bf16[1,16,2560]{2,1,0:T(8,128)(2,1)S(1)}, bf16[1,16,2560]{2,1,0:T(8,128)(2,1)}, u32[]{:S(2)}) copy-start(bf16[1,16,2560]{2,1,0:T(8,128)(2,1)} %param.12) | copy-start | bytes 245764
  109.5 148.7 %all-gather.6.cloned.1.call-start = ((), (), s32[]{:S(2)}) async-start(), calls=%async_computation.3 | async-start | bytes 2703360 | tf_op jit(solution)/shard_map/all_gather | solution.py:45
  205.5 96.6 %reduce-scatter.5.cloned.1.call-start = ((), (), s32[]{:S(2)}) async-start(), calls=%async_computation.4 | async-start | bytes 2359296 | tf_op jit(solution)/shard_map/reduce_scatter | solution.py:52
  264.8 38.7 %copy-start.1 = (bf16[1,512,2560]{2,1,0:T(8,128)(2,1)S(1)}, bf16[1,512,2560]{2,1,0:T(8,128)(2,1)}, u32[]{:S(2)}) copy-start(bf16[1,512,2560]{2,1,0:T(8,128)(2,1)} %all-gather.8.cloned.1.call-done) | copy-start | bytes 7864324
Sparse Core Ops, SparseCore 0:
  10.6 53.7 all-gather.7
  67.7 32.6 all-gather.9
  109.6 94.1 reduce-scatter.2
  207.1 50.9 all-gather.5
  265.0 37.0 reduce-scatter.4
where the time goes:
time: 317 us; the launch traced here: 314 us
  waiting for transfers between devices  265 us (84%)
  matrix products  26.4 us (8%)
  between operations  13.8 us (4%)
  local copies, waits for them, and re-layouts  5.05 us (2%)
  other arithmetic  3.27 us (1%)
    reduce_scatter x1, waiting for transfers between devices, body(): lax.psum_scatter(jnp.einsum('ltf,lfd->td', code_rows, local_dec, preferre...  93.6 us
    all_gather x1, waiting for transfers between devices, body(): whole_inputs = lax.all_gather(inputs[0], 'feat', axis=0, tiled=True)  55.5 us
    all_gather x1, waiting for transfers between devices, body(): rows_in = lax.all_gather(residual_part, 'feat', axis=0, tiled=True)  52.7 us
    all_gather x1, waiting for transfers between devices, body(): visible = lax.all_gather(code_vals[None], 'section', axis=0, tiled=True)  32.7 us
    reduce_scatter x1, waiting for transfers between devices, body(): lax.psum_scatter(code_grad, 'section', scatter_dimension=0, tiled=True)[0]  29.7 us
    dot_general x1, matrix products, body(): jnp.einsum('ltf,lfd->td', code_rows, local_dec, preferred_element_type=jn...  7.61 us
    dot_general x1, matrix products, body(): jnp.einsum('ltf,td->lfd', code_rows, rows_in, preferred_element_type=jnp....  7.49 us
    dot_general x1, matrix products, body(): jnp.einsum('td,lfd->ltf', rows_in, local_dec, preferred_element_type=jnp....  6.64 us
  transfers between devices with their start and end apart: 5, of which 5 were waited for; matrix products, arithmetic and copies ran while one was open for 3% of the time, Pallas kernels for 0%

commit v1 on v0

v1 whole, which is shorter than its diff:
```python
import functools

import jax
import jax.numpy as jnp
from jax import lax
from jax.experimental import pallas as pl
from jax.experimental.pallas import tpu as pltpu
from jax.sharding import PartitionSpec as P

MESH = pl.DeviceIdType.MESH
BF16 = jnp.bfloat16
F32 = jnp.float32

NX = 4
NY = 4
CHIPS = NX * NY
NZ = 8
ROWS = 16
FW = 128
D = 2560
TOK = CHIPS * ROWS
PAIR = 2 * FW
HALF = TOK // 2
TILE = 512

PLANE = [(dx, dy) for dx in range(NX) for dy in range(NY) if (dx, dy) != (0, 0)]
PLANE.sort(key=lambda o: -(min(o[0], NX - o[0]) + min(o[1], NY - o[1])))


def step_kernel(
    x_ref, we_ref, be_ref, wd_ref, bd_ref, tg_ref, act_ref,
    xo_ref, ro_ref, co_ref, pg_ref,
    xg, rg, we_s, wd_s, be_s, be_t, vis, live, acc, rb, rsr, cs, pg_s, zsb, zrb,
    in_sem, in_ssem, in_rsem, a_ssem, a_rsem, b_ssem, b_rsem, c_ssem, c_rsem,
    e_ssem, e_rsem, g_ssem, g_rsem, p_ssem, p_rsem, out_sem,
):
    s = lax.axis_index("section")
    f = lax.axis_index("feat")
    core = lax.rem(f, 2)
    chip = lax.div(f, 2)
    cx = lax.div(chip, NY)
    cy = lax.rem(chip, NY)

    def plane_chip(o):
        return lax.rem(cx + o[0], NX) * NY + lax.rem(cy + o[1], NY)

    def plane_dev(o):
        return {"section": s, "feat": plane_chip(o) * 2 + core}

    peer = {"section": s, "feat": chip * 2 + 1 - core}
    up = {"section": lax.rem(s + 1, NZ), "feat": f}
    down = {"section": lax.rem(s + NZ - 1, NZ), "feat": f}

    def remote(src, dst, ssem, rsem, dev):
        return pltpu.make_async_remote_copy(
            src_ref=src, dst_ref=dst, send_sem=ssem, recv_sem=rsem, device_id=dev, device_id_type=MESH
        )

    barrier = pltpu.get_barrier_semaphore()
    for dev in [peer, up, down] + [plane_dev(o) for o in PLANE]:
        pl.semaphore_signal(barrier, inc=1, device_id=dev, device_id_type=MESH)

    loc = [pltpu.make_async_copy(we_ref, we_s.at[:, pl.ds(0, FW)], in_sem.at[NZ])]
    for l in range(NZ):
        loc.append(pltpu.make_async_copy(wd_ref.at[l], wd_s.at[l, pl.ds(0, FW)], in_sem.at[l]))
    for cp in loc:
        cp.start()
    be_t[...] = jnp.broadcast_to(be_ref[...], (8, FW))
    xg[0, chip] = x_ref[...]

    pl.semaphore_wait(barrier, 3 + len(PLANE))

    ag_x = [
        remote(x_ref, xg.at[0, chip], a_ssem.at[k], a_rsem.at[k], plane_dev(o)) for k, o in enumerate(PLANE)
    ]
    for cp in ag_x:
        cp.start()
    swap = [
        remote(we_ref, we_s.at[:, pl.ds(FW, FW)], in_ssem.at[NZ], in_rsem.at[NZ], peer),
        remote(be_t, be_s, in_ssem.at[NZ + 1], in_rsem.at[NZ + 1], peer),
    ]
    for l in range(NZ):
        swap.append(remote(wd_ref.at[l], wd_s.at[l, pl.ds(FW, FW)], in_ssem.at[l], in_rsem.at[l], peer))
    for cp in swap:
        cp.start()

    act = act_ref[...]
    row_chip = lax.broadcasted_iota(jnp.int32, (TOK, CHIPS), 0) // ROWS
    expand = (row_chip == lax.broadcasted_iota(jnp.int32, (TOK, CHIPS), 1)).astype(F32)

    def keep_of(block):
        hit = jnp.max((act == block).astype(F32), axis=1, keepdims=True)
        return jnp.dot(expand, jnp.broadcast_to(hit, (CHIPS, FW)), preferred_element_type=F32)

    live[:, 0:FW] = keep_of(f)
    live[:, FW:PAIR] = keep_of(chip * 2 + 1 - core)

    loc[0].wait()
    swap[0].wait_recv()
    swap[1].wait_recv()
    for cp in ag_x:
        cp.wait_recv()

    pre = jnp.dot(xg[0].reshape(TOK, D), we_s[...], preferred_element_type=F32)
    bias = jnp.concatenate([be_t[0:1, :], be_s[0:1, :]], axis=1)
    pre = pre + bias
    mask = live[...] * (pre > 0).astype(F32)
    live[...] = mask
    vis[s] = (mask * pre).astype(BF16)

    def zcopy(way, hop, half):
        block = lax.rem(s - hop + 1 + NZ, NZ) if way == 0 else lax.rem(s + hop - 1, NZ)
        ref = vis.at[block, pl.ds(half * HALF, HALF)]
        return remote(ref, ref, b_ssem.at[way, hop - 1, half], b_rsem.at[way, hop - 1, half], up if way == 0 else down)

    def zhalves(way, hop):
        return (0, 1) if hop < 4 else (way,)

    zsends = {}
    for half in (0, 1):
        for way in (0, 1):
            cp = zcopy(way, 1, half)
            cp.start()
            zsends[way, 1, half] = cp

    swap_x = remote(xg.at[0], xg.at[1], p_ssem.at[0], p_rsem.at[0], peer)
    swap_x.start()

    for l in range(NZ):
        loc[1 + l].wait()
        swap[2 + l].wait_recv()

    def add_block(block, first=False):
        @pl.loop(0, D // TILE)
        def _(j):
            col = pl.ds(pl.multiple_of(j * TILE, TILE), TILE)
            part = jnp.dot(vis[block], wd_s[block, :, col], preferred_element_type=F32)
            if first:
                acc[:, col] = part
            else:
                acc[:, col] += part

    add_block(s, True)
    for hop in (1, 2, 3):
        for half in (0, 1):
            for way in (0, 1):
                zsends[way, hop, half].wait_recv()
                if half in zhalves(way, hop + 1):
                    cp = zcopy(way, hop + 1, half)
                    cp.start()
                    zsends[way, hop + 1, half] = cp

        @pl.when(s >= hop)
        def _():
            add_block(lax.rem(s - hop + NZ, NZ))

        @pl.when(s + hop >= NZ)
        def _():
            add_block(lax.rem(s + hop, NZ))

    for way in (0, 1):
        zsends[way, 4, way].wait_recv()

    @pl.when(s >= 4)
    def _():
        add_block(lax.rem(s + 4, NZ))

    for i in range(CHIPS):
        rb[i] = acc[i * ROWS:(i + 1) * ROWS, :].astype(BF16)
    rs = [
        remote(rb.at[plane_chip(o)], rsr.at[chip], c_ssem.at[k], c_rsem.at[k], plane_dev(o))
        for k, o in enumerate(PLANE)
    ]
    for cp in rs:
        cp.start()
    swap_c = remote(vis.at[:, :, pl.ds(FW, FW)], cs.at[:, 1], p_ssem.at[1], p_rsem.at[1], peer)
    swap_c.start()
    total = acc[pl.ds(pl.multiple_of(chip * ROWS, ROWS), ROWS), :] + bd_ref[...].astype(F32) - tg_ref[...].astype(F32)
    cs[:, 0] = vis[:, :, 0:FW]
    for k, o in enumerate(PLANE):
        rs[k].wait_recv()
        src = lax.rem(cx + NX - o[0], NX) * NY + lax.rem(cy + NY - o[1], NY)
        total = total + rsr[src].astype(F32)
    rg[0, chip] = total.astype(BF16)

    ag_r = [
        remote(rg.at[0, chip], rg.at[0, chip], e_ssem.at[k], e_rsem.at[k], plane_dev(o)) for k, o in enumerate(PLANE)
    ]
    for cp in ag_r:
        cp.start()
    swap_x.wait_recv()
    out_x = pltpu.make_async_copy(xg, xo_ref, out_sem.at[0])
    out_x.start()
    swap_c.wait_recv()
    out_c = pltpu.make_async_copy(cs, co_ref, out_sem.at[1])
    out_c.start()
    for cp in ag_r:
        cp.wait_recv()
    swap_r = remote(rg.at[0], rg.at[1], p_ssem.at[2], p_rsem.at[2], peer)
    swap_r.start()

    def code_grad(block):
        return lax.dot_general(
            rg[0].reshape(TOK, D), wd_s[block], (((1,), (1,)), ((), ())), preferred_element_type=F32
        )

    def gcopy(way, j, half):
        return remote(
            zsb.at[way, j - 1, half], zrb.at[way, j - 1, half],
            g_ssem.at[way, j - 1, half], g_rsem.at[way, j - 1, half], down if way == 0 else up,
        )

    gsends = {}
    for j in (4, 3, 2, 1):
        for way in (0, 1):
            if way == 0:
                block, given = lax.rem(s - j + NZ, NZ), s >= j
            else:
                block, given = lax.rem(s + j, NZ), s + j >= NZ
            if j == 4:
                if way == 0:
                    acc[:, 0:PAIR] = jnp.where(given, code_grad(block), 0.0)
                part = acc[way * HALF:(way + 1) * HALF, 0:PAIR]
                parts = {way: part}
            else:
                acc[:, 0:PAIR] = jnp.where(given, code_grad(block), 0.0)
                parts = {h: acc[h * HALF:(h + 1) * HALF, 0:PAIR] for h in (way, 1 - way)}
            for half, part in parts.items():
                if (way, j + 1, half) in gsends:
                    gsends[way, j + 1, half].wait_recv()
                    part = part + zrb[way, j, half].astype(F32)
                zsb[way, j - 1, half] = part.astype(BF16)
                cp = gcopy(way, j, half)
                cp.start()
                gsends[way, j, half] = cp

    acc[:, 0:PAIR] = code_grad(s)
    swap_r.wait_recv()
    out_r = pltpu.make_async_copy(rg, ro_ref, out_sem.at[2])
    out_r.start()
    for half in (0, 1):
        rows = slice(half * HALF, (half + 1) * HALF)
        own = acc[rows, 0:PAIR]
        for way in (0, 1):
            gsends[way, 1, half].wait_recv()
            own = own + zrb[way, 0, half].astype(F32)
        grad = (own * live[rows, :]).astype(BF16)
        pg_s[0, 0, rows, :] = grad[:, 0:FW]
        pg_s[1, 0, rows, :] = grad[:, FW:PAIR]
    swap_g = remote(pg_s.at[1, 0], pg_s.at[0, 1], p_ssem.at[3], p_rsem.at[3], peer)
    swap_g.start()
    swap_g.wait_recv()
    pg_ref[...] = pg_s[0]

    for cp in ag_x + ag_r + rs + swap + [swap_x, swap_c, swap_r, swap_g]:
        cp.wait_send()
    for cp in list(zsends.values()) + list(gsends.values()):
        cp.wait_send()
    out_x.wait()
    out_c.wait()
    out_r.wait()


def fused(x, we, be, wd, bd, tg, act):
    vmem = pl.BlockSpec(memory_space=pltpu.VMEM)
    hbm = pl.BlockSpec(memory_space=pl.ANY)
    dma = pltpu.SemaphoreType.DMA
    n = len(PLANE)
    return pl.pallas_call(
        step_kernel,
        name="step",
        out_shape=(
            jax.ShapeDtypeStruct((2, CHIPS, ROWS, D), BF16),
            jax.ShapeDtypeStruct((2, CHIPS, ROWS, D), BF16),
            jax.ShapeDtypeStruct((NZ, 2, TOK, FW), BF16),
            jax.ShapeDtypeStruct((2, TOK, FW), BF16),
        ),
        in_specs=[vmem, hbm, vmem, hbm, vmem, vmem, vmem],
        out_specs=(hbm, hbm, hbm, vmem),
        scratch_shapes=[
            pltpu.VMEM((2, CHIPS, ROWS, D), BF16),
            pltpu.VMEM((2, CHIPS, ROWS, D), BF16),
            pltpu.VMEM((D, PAIR), BF16),
            pltpu.VMEM((NZ, PAIR, D), BF16),
            pltpu.VMEM((8, FW), F32),
            pltpu.VMEM((8, FW), F32),
            pltpu.VMEM((NZ, TOK, PAIR), BF16),
            pltpu.VMEM((TOK, PAIR), F32),
            pltpu.VMEM((TOK, D), F32),
            pltpu.VMEM((CHIPS, ROWS, D), BF16),
            pltpu.VMEM((CHIPS, ROWS, D), BF16),
            pltpu.VMEM((NZ, 2, TOK, FW), BF16),
            pltpu.VMEM((2, 2, TOK, FW), BF16),
            pltpu.VMEM((2, 4, 2, HALF, PAIR), BF16),
            pltpu.VMEM((2, 4, 2, HALF, PAIR), BF16),
            dma((NZ + 1,)), dma((NZ + 2,)), dma((NZ + 2,)),
            dma((n,)), dma((n,)),
            dma((2, 4, 2)), dma((2, 4, 2)),
            dma((n,)), dma((n,)),
            dma((n,)), dma((n,)),
            dma((2, 4, 2)), dma((2, 4, 2)),
            dma((4,)), dma((4,)),
            dma((3,)),
        ],
        compiler_params=pltpu.CompilerParams(
            collective_id=0, has_side_effects=True, vmem_limit_bytes=56 * 2**20
        ),
    )(x, we, be, wd, bd, tg, act)


def body(inputs, enc_weight, enc_bias, dec_weight, dec_bias, target, active):
    xa, ra, codes, pg = fused(
        inputs[0], enc_weight[0], enc_bias, dec_weight[0], dec_bias, target[0], active[0]
    )
    xa = xa.reshape(2 * TOK, D)
    ra = ra.reshape(2 * TOK, D)
    codes = codes.reshape(NZ, 2 * TOK, FW)
    pg = pg.reshape(2 * TOK, FW)
    causal = (lax.iota(jnp.int32, NZ) <= lax.axis_index("section")).astype(BF16)
    codes = codes * causal[:, None, None]
    enc_grad = jnp.einsum("td,tf->df", xa, pg, preferred_element_type=F32).astype(BF16)
    bias_grad = jnp.sum(pg.astype(F32), axis=0)
    dec_grad = jnp.einsum("ltf,td->lfd", codes, ra, preferred_element_type=F32).astype(BF16)
    return enc_grad[None], bias_grad[None], dec_grad[None]


def solution(mesh):
    return jax.shard_map(
        body,
        mesh=mesh,
        in_specs=(
            P("section", "feat", None),
            P("section", None, "feat"),
            P("section", "feat"),
            P("section", None, "feat", None),
            P("section", None),
            P("section", "feat", None),
            P("section", None, None),
        ),
        out_specs=(
            P("section", None, "feat"),
            P("section", "feat"),
            P("section", None, "feat", None),
        ),
        check_vma=False,
    )
```

time: 317 us -> 110 us (0.35)
  waiting for transfers between devices: 265 us -> 0 us
  Pallas kernels: 0 us -> 98.6 us
  matrix products: 26.4 us -> 8.29 us
  between operations: 13.8 us -> 0.69 us
  local copies, waits for them, and re-layouts: 5.05 us -> 1.37 us
    all_gather x3 -> x0, waiting for transfers between devices: 141 us -> none  [the longest x1 55.5 us: body(): whole_inputs = lax.all_gather(inputs[0], 'feat', axis=0, tiled=True)]
    reduce_scatter x2 -> x0, waiting for transfers between devices: 123 us -> none  [the longest x1 93.6 us: body(): lax.psum_scatter(jnp.einsum('ltf,lfd->td', code_rows, local_dec, preferre...]
    pallas_call x0 -> x1, Pallas kernels: none -> 98.6 us  [fused(): pl.pallas_call(step_kernel, name='step', out_shape=(jax.ShapeDtypeStruct(...]
    dot_general x5 -> x2, matrix products: 26.4 us -> 8.29 us  [the longest x1 4.66 us: body(): jnp.einsum('ltf,td->lfd', codes, ra, preferred_element_type=F32)]
  transfers between devices with their start and end apart: 5 -> 0, of which waited for: 5 -> 0; matrix products, arithmetic and copies ran while one was open for 3% -> 0% of each run, Pallas kernels for 0% -> 0%
where the time goes in v1:
time: 110 us
  Pallas kernels  98.6 us (90%)
  matrix products  8.29 us (8%)
  local copies, waits for them, and re-layouts  1.37 us (1%)
    pallas_call x1, Pallas kernels, fused(): pl.pallas_call(step_kernel, name='step', out_shape=(jax.ShapeDtypeStruct(...  98.6 us
    dot_general x1, matrix products, body(): jnp.einsum('ltf,td->lfd', codes, ra, preferred_element_type=F32)  4.66 us
    dot_general x1, matrix products, body(): jnp.einsum('td,tf->df', xa, pg, preferred_element_type=F32).astype(BF16)  3.63 us

profile of v1, /device:TPU:1, one launch (start us, length us, event | category | flops | bytes accessed | tf_op | source)
XLA Modules:
  0.0 109.7 jit_solution(3653978329714899847)
XLA Ops:
  0.6 1.4 %copy.10.act_ref = s32[16,8]{1,0:T(8,128)} copy(s32[16,8]{0,1:T(8,128)} %bitcast.27) | data formatting | bytes 1024 | tf_op jit(solution)/shard_map/squeeze | solution.py:313
  2.0 98.6 %step.1 = (bf16[2,16,16,2560]{3,2,1,0:T(8,128)(2,1)}, bf16[2,16,16,2560]{3,2,1,0:T(8,128)(2,1)}, bf16[8,2,256,128]{3,2,1,0:T(8,128)(2,1)}, bf16[2,256,128]{2,1,0:T(8,128)(2,1)}) custom-call(bf16[16,2560]{1,0:T(8,128)(2,1)} %bitcast.25, bf16[2560,128]{1,0:T(8,128)(2,1)} %bitcast.23, f32[1,128]{1,0:T(1,128)} %be_ref.1, bf16[8,128,2560]{2,1,0:T(8,128)(2,1)} %bitcast.21, ...), custom_call_target="tpu_custom_call" | custom-call | tf_op jit(solution)/shard_map/step/pallas_call | solution.py:269
  100.6 0.0 copy-start.1
  100.6 0.0 copy-start
  100.6 0.0 copy-start.2
  100.6 3.6 %fusion.1 = bf16[1,2560,128]{2,1,0:T(8,128)(2,1)} fusion(bf16[512,2560]{1,0:T(8,128)(2,1)} %bitcast.20, bf16[512,128]{1,0:T(8,128)(2,1)} %bitcast.24), kind=kOutput, calls=%fused_computation.3 | convolution fusion | flops 335872000 | bytes 3407872 | tf_op jit(solution)/shard_map/td,tf->df/dot_general | solution.py:321
  104.3 0.0 copy-done.1
  104.3 0.6 convert_reduce_fusion
  104.9 0.0 copy-done
  104.9 0.1 broadcast_multiply_fusion
  105.0 0.0 copy-done.2
  105.0 4.7 %fusion = bf16[1,8,128,2560]{3,2,1,0:T(8,128)(2,1)} fusion(bf16[8,512,128]{2,1,0:T(8,128)(2,1)S(1)} %bitcast.22, bf16[512,2560,1]{1,0,2:T(8,128)(2,1)S(1)} %bitcast.29), kind=kOutput, calls=%fused_computation.1 | convolution fusion | flops 2686976000 | bytes 8912896 | tf_op jit(solution)/shard_map/ltf,td->lfd/dot_general | solution.py:323
  (1 shorter events, 0.0 us)
Async XLA Ops:
  100.6 3.7 %copy-start.1 = (bf16[2,256,128]{2,1,0:T(8,128)(2,1)S(1)}, bf16[2,256,128]{2,1,0:T(8,128)(2,1)}, u32[]{:S(2)}) copy-start(bf16[2,256,128]{2,1,0:T(8,128)(2,1)} %get-tuple-element.8) | copy-start | bytes 393220
  100.6 4.2 %copy-start = (bf16[8,2,256,128]{3,2,1,0:T(8,128)(2,1)S(1)}, bf16[8,2,256,128]{3,2,1,0:T(8,128)(2,1)}, u32[]{:S(2)}) copy-start(bf16[8,2,256,128]{3,2,1,0:T(8,128)(2,1)} %get-tuple-element.9) | copy-start | bytes 3145732
  100.6 4.4 %copy-start.2 = (bf16[2,16,16,2560]{3,2,1,0:T(8,128)(2,1)S(1)}, bf16[2,16,16,2560]{3,2,1,0:T(8,128)(2,1)}, u32[]{:S(2)}) copy-start(bf16[2,16,16,2560]{3,2,1,0:T(8,128)(2,1)} %get-tuple-element.10) | copy-start | bytes 7864324

commit v2 on v1

v2 whole, which is shorter than its diff:
```python
import functools

import jax
import jax.numpy as jnp
from jax import lax
from jax.experimental import pallas as pl
from jax.experimental.pallas import tpu as pltpu
from jax.sharding import PartitionSpec as P

MESH = pl.DeviceIdType.MESH
BF16 = jnp.bfloat16
F32 = jnp.float32

NX = 4
NY = 4
CHIPS = NX * NY
NZ = 8
ROWS = 16
FW = 128
D = 2560
TOK = CHIPS * ROWS
PAIR = 2 * FW
HALF = TOK // 2
TILE = 512

HD = D // 2
LEFT = pl.ds(0, HD)
RIGHT = pl.ds(HD, HD)


def step_kernel(
    x_ref, we_ref, be_ref, wd_ref, bd_ref, tg_ref, act_ref,
    eg_ref, bg_ref, dg_ref,
    xg, rg, we_s, wd_s, be_s, bd_s, tg_s, act_s, vis, live, acc, rb, r1, r2s, r2, tot, cs, ct, xt, pg_s, zsb, zrb,
    in_sem, in_ssem, in_rsem, a_ssem, a_rsem, b_ssem, b_rsem, c_ssem, c_rsem,
    e_ssem, e_rsem, g_ssem, g_rsem, p_ssem, p_rsem, small_sem,
):
    s = lax.axis_index("section")
    f = lax.axis_index("feat")
    core = lax.rem(f, 2)
    chip = lax.div(f, 2)
    cx = lax.div(chip, NY)
    cy = lax.rem(chip, NY)

    def along(axis, step):
        x = lax.rem(cx + step, NX) if axis == 0 else cx
        y = lax.rem(cy + step, NY) if axis == 1 else cy
        return {"section": s, "feat": (x * NY + y) * 2 + core}

    peer = {"section": s, "feat": chip * 2 + 1 - core}
    up = {"section": lax.rem(s + 1, NZ), "feat": f}
    down = {"section": lax.rem(s + NZ - 1, NZ), "feat": f}
    up2 = {"section": lax.rem(s + 2, NZ), "feat": f}
    down2 = {"section": lax.rem(s + NZ - 2, NZ), "feat": f}

    def remote(src, dst, ssem, rsem, dev):
        return pltpu.make_async_remote_copy(
            src_ref=src, dst_ref=dst, send_sem=ssem, recv_sem=rsem, device_id=dev, device_id_type=MESH
        )

    barrier = pltpu.get_barrier_semaphore()
    for dev in [peer, up, down, up2, down2] + [along(axis, o) for axis in (0, 1) for o in (1, 2, 3)]:
        pl.semaphore_signal(barrier, inc=1, device_id=dev, device_id_type=MESH)

    loc = [pltpu.make_async_copy(we_ref, we_s.at[:, pl.ds(0, FW)], in_sem.at[NZ])]
    for l in range(NZ):
        loc.append(pltpu.make_async_copy(wd_ref.at[l], wd_s.at[l, pl.ds(0, FW)], in_sem.at[l]))
    small = [
        pltpu.make_async_copy(a, b, small_sem.at[k])
        for k, (a, b) in enumerate(
            [(act_ref, act_s), (be_ref, be_s.at[0]), (x_ref, xg.at[0, 0, 0]), (bd_ref, bd_s), (tg_ref, tg_s)]
        )
    ]
    for cp in small + loc:
        cp.start()

    pl.semaphore_wait(barrier, 11)

    def gather_first(src, g, ssem, rsem):
        copies = {}
        for o in (2, 1, 3):
            for axis in (0, 1):
                there = (NX - o, 0) if axis == 0 else (0, NY - o)
                cp = remote(src, g.at[0, there[0], there[1]], ssem.at[0, axis, o - 1], rsem.at[0, axis, o - 1], along(axis, o))
                cp.start()
                copies[axis, o] = cp
        return copies

    def gather_second(first, g, ssem, rsem):
        copies = []
        for axis in (0, 1):
            for o in (1, 3, 2):
                first[axis, o].wait_recv()
            for o in (2, 1, 3):
                if axis == 0:
                    src, dst = g.at[0, pl.ds(1, 3), 0, :, LEFT], g.at[0, pl.ds(1, 3), NY - o, :, LEFT]
                else:
                    src, dst = g.at[0, 0, pl.ds(1, 3), :, RIGHT], g.at[0, NX - o, pl.ds(1, 3), :, RIGHT]
                cp = remote(src, dst, ssem.at[1, axis, o - 1], rsem.at[1, axis, o - 1], along(1 - axis, o))
                cp.start()
                copies.append(cp)
        return copies

    ag_x1 = gather_first(x_ref, xg, a_ssem, a_rsem)
    swap = [
        remote(we_ref, we_s.at[:, pl.ds(FW, FW)], in_ssem.at[NZ], in_rsem.at[NZ], peer),
        remote(be_ref, be_s.at[1], in_ssem.at[NZ + 1], in_rsem.at[NZ + 1], peer),
    ]
    for l in range(NZ):
        swap.append(remote(wd_ref.at[l], wd_s.at[l, pl.ds(FW, FW)], in_ssem.at[l], in_rsem.at[l], peer))
    for cp in swap:
        cp.start()

    small[0].wait()
    act = act_s[...]
    row_at = lax.broadcasted_iota(jnp.int32, (TOK, CHIPS), 0) // ROWS
    row_chip = lax.rem(cx + row_at // NY, NX) * NY + lax.rem(cy + lax.rem(row_at, NY), NY)
    expand = (row_chip == lax.broadcasted_iota(jnp.int32, (TOK, CHIPS), 1)).astype(F32)

    def keep_of(block):
        hit = jnp.max((act == block).astype(F32), axis=0, keepdims=True)
        return jnp.broadcast_to(jnp.sum(expand * hit, axis=1, keepdims=True), (TOK, FW))

    live[:, 0:FW] = keep_of(f)
    live[:, FW:PAIR] = keep_of(chip * 2 + 1 - core)

    ag_x = gather_second(ag_x1, xg, a_ssem, a_rsem)
    small[1].wait()
    small[2].wait()
    loc[0].wait()
    swap[0].wait_recv()
    swap[1].wait_recv()
    for cp in ag_x:
        cp.wait_recv()

    pre = jnp.dot(xg[0].reshape(TOK, D), we_s[...], preferred_element_type=F32)
    bias = jnp.concatenate([be_s[0], be_s[1]], axis=1)
    pre = pre + bias
    mask = live[...] * (pre > 0).astype(F32)
    live[...] = mask
    vis[s] = (mask * pre).astype(BF16)

    def zcopy(way, hop, half):
        held = 2 if hop == 4 else hop - 1
        block = lax.rem(s - held + NZ, NZ) if way == 0 else lax.rem(s + held, NZ)
        ref = vis.at[block, pl.ds(half * HALF, HALF)]
        dev = ((up, up2), (down, down2))[way][hop == 4]
        return remote(ref, ref, b_ssem.at[way, hop - 1, half], b_rsem.at[way, hop - 1, half], dev)

    zsends = {}
    for half in (0, 1):
        for way in (0, 1):
            cp = zcopy(way, 1, half)
            cp.start()
            zsends[way, 1, half] = cp

    swap_x = remote(xg.at[0], xg.at[1], p_ssem.at[0], p_rsem.at[0], peer)
    swap_x.start()

    for l in range(NZ):
        loc[1 + l].wait()
        swap[2 + l].wait_recv()

    def add_block(block, first=False):
        @pl.loop(0, D // TILE)
        def _(j):
            col = pl.ds(pl.multiple_of(j * TILE, TILE), TILE)
            part = jnp.dot(vis[block], wd_s[block, :, col], preferred_element_type=F32)
            if first:
                acc[:, col] = part
            else:
                acc[:, col] += part

    add_block(s, True)
    for hop in (1, 2, 3):
        for half in (0, 1):
            for way in (0, 1):
                zsends[way, hop, half].wait_recv()
                for later in ((2,), (3, 4) if half == way else (3,), ())[hop - 1]:
                    cp = zcopy(way, later, half)
                    cp.start()
                    zsends[way, later, half] = cp

        @pl.when(s >= hop)
        def _():
            add_block(lax.rem(s - hop + NZ, NZ))

        @pl.when(s + hop >= NZ)
        def _():
            add_block(lax.rem(s + hop, NZ))

    for way in (0, 1):
        zsends[way, 4, way].wait_recv()

    rs1 = {}
    for axis in (0, 1):
        cols = slice(axis * HD, (axis + 1) * HD)

        @pl.when(s >= 4)
        def _():
            block = lax.rem(s + 4, NZ)
            acc[:, cols] += jnp.dot(vis[block], wd_s[block, :, cols], preferred_element_type=F32)

        rb[:, :, :, cols] = acc[:, cols].astype(BF16).reshape(NX, NY, ROWS, HD)
        for o in (2, 1, 3):
            src = rb.at[o, :, :, LEFT] if axis == 0 else rb.at[:, o, :, RIGHT]
            cp = remote(src, r1.at[axis, o - 1], c_ssem.at[0, axis, o - 1], c_rsem.at[0, axis, o - 1], along(axis, o))
            cp.start()
            rs1[axis, o] = cp
    swap_c = remote(vis.at[:, :, pl.ds(FW, FW)], cs.at[:, 1], p_ssem.at[1], p_rsem.at[1], peer)
    swap_c.start()
    cs[:, 0] = vis[:, :, 0:FW]
    xt[:, 0:TOK] = xg[0].reshape(TOK, D).T
    rs2 = {}
    for axis in (0, 1):
        for o in (1, 3, 2):
            rs1[axis, o].wait_recv()
        for o in (2, 1, 3, 0):
            at = o if axis == 0 else o * NY
            part = acc[at * ROWS:(at + 1) * ROWS, axis * HD:(axis + 1) * HD]
            for k in range(3):
                part = part + r1[axis, k, o].astype(F32)
            if o == 0:
                tot[:, axis * HD:(axis + 1) * HD] = part
            else:
                r2s[axis, o - 1] = part.astype(BF16)
                cp = remote(
                    r2s.at[axis, o - 1], r2.at[axis, o - 1], c_ssem.at[1, axis, o - 1], c_rsem.at[1, axis, o - 1], along(1 - axis, o)
                )
                cp.start()
                rs2[axis, o] = cp
    small[3].wait()
    small[4].wait()
    tot[...] += bd_s[...].astype(F32) - tg_s[...].astype(F32)
    for axis in (0, 1):
        part = tot[:, axis * HD:(axis + 1) * HD]
        for o in (1, 3, 2):
            rs2[axis, o].wait_recv()
            part = part + r2[axis, o - 1].astype(F32)
        rg[0, 0, 0, :, axis * HD:(axis + 1) * HD] = part.astype(BF16)

    ag_r1 = gather_first(rg.at[0, 0, 0], rg, e_ssem, e_rsem)
    ag_r = gather_second(ag_r1, rg, e_ssem, e_rsem)
    swap_x.wait_recv()
    xt[:, TOK:2 * TOK] = xg[1].reshape(TOK, D).T
    swap_c.wait_recv()
    for l in range(NZ):
        seen = cs[l].reshape(2 * TOK, FW).T
        ct[l] = jnp.where(s >= l, seen, jnp.zeros_like(seen))
    for cp in ag_r:
        cp.wait_recv()
    swap_r = remote(rg.at[0], rg.at[1], p_ssem.at[2], p_rsem.at[2], peer)
    swap_r.start()

    def code_grad(block):
        return lax.dot_general(
            rg[0].reshape(TOK, D), wd_s[block], (((1,), (1,)), ((), ())), preferred_element_type=F32
        )

    def gcopy(way, j, half):
        return remote(
            zsb.at[way, j - 1, half], zrb.at[way, j - 1, half],
            g_ssem.at[way, j - 1, half], g_rsem.at[way, j - 1, half], ((down, down2), (up, up2))[way][j == 4],
        )

    gsends = {}
    for j in (4, 3, 2, 1):
        for way in (0, 1):
            if way == 0:
                block, given = lax.rem(s - j + NZ, NZ), s >= j
            else:
                block, given = lax.rem(s + j, NZ), s + j >= NZ
            if j == 4:
                if way == 0:
                    acc[:, 0:PAIR] = jnp.where(given, code_grad(block), 0.0)
                part = acc[way * HALF:(way + 1) * HALF, 0:PAIR]
                parts = {way: part}
            else:
                acc[:, 0:PAIR] = jnp.where(given, code_grad(block), 0.0)
                parts = {h: acc[h * HALF:(h + 1) * HALF, 0:PAIR] for h in (way, 1 - way)}
            for half, part in parts.items():
                for k in {2: (4, 3) if half == way else (3,), 1: (2,)}.get(j, ()):
                    gsends[way, k, half].wait_recv()
                    part = part + zrb[way, k - 1, half].astype(F32)
                zsb[way, j - 1, half] = part.astype(BF16)
                cp = gcopy(way, j, half)
                cp.start()
                gsends[way, j, half] = cp

    acc[:, 0:PAIR] = code_grad(s)
    swap_r.wait_recv()
    outs = []
    for j in range(D // TILE):
        col = slice(j * TILE, (j + 1) * TILE)
        part = jnp.dot(
            ct[...].reshape(NZ * FW, 2 * TOK), rg[...].reshape(2 * TOK, D)[:, col], preferred_element_type=F32
        )
        dg_ref[:, :, col] = part.astype(BF16).reshape(NZ, FW, TILE)
    for half in (0, 1):
        rows = slice(half * HALF, (half + 1) * HALF)
        own = acc[rows, 0:PAIR]
        for way in (0, 1):
            gsends[way, 1, half].wait_recv()
            own = own + zrb[way, 0, half].astype(F32)
        grad = (own * live[rows, :]).astype(BF16)
        pg_s[0, 0, rows, :] = grad[:, 0:FW]
        pg_s[1, 0, rows, :] = grad[:, FW:PAIR]
    swap_g = remote(pg_s.at[1, 0], pg_s.at[0, 1], p_ssem.at[3], p_rsem.at[3], peer)
    swap_g.start()
    swap_g.wait_recv()
    pg = pg_s[0].reshape(2 * TOK, FW)
    eg_ref[...] = jnp.dot(xt[...], pg, preferred_element_type=F32).astype(BF16)
    bg_ref[...] = jnp.sum(pg.astype(F32), axis=0, keepdims=True)

    for cp in list(ag_x1.values()) + list(ag_r1.values()) + list(rs1.values()) + list(rs2.values()):
        cp.wait_send()
    for cp in ag_x + ag_r + swap + [swap_x, swap_c, swap_r, swap_g]:
        cp.wait_send()
    for cp in list(zsends.values()) + list(gsends.values()):
        cp.wait_send()
    for cp in outs:
        cp.wait()


def fused(x, we, be, wd, bd, tg, act):
    vmem = pl.BlockSpec(memory_space=pltpu.VMEM)
    hbm = pl.BlockSpec(memory_space=pl.ANY)
    dma = pltpu.SemaphoreType.DMA
    return pl.pallas_call(
        step_kernel,
        name="step",
        out_shape=(
            pltpu.VMEM((D, FW), BF16),
            pltpu.VMEM((1, FW), F32),
            pltpu.VMEM((NZ, FW, D), BF16),
        ),
        in_specs=[pl.BlockSpec(memory_space=pltpu.HBM)] * 7,
        out_specs=(vmem, vmem, vmem),
        scratch_shapes=[
            pltpu.VMEM((2, NX, NY, ROWS, D), BF16),
            pltpu.VMEM((2, NX, NY, ROWS, D), BF16),
            pltpu.VMEM((D, PAIR), BF16),
            pltpu.VMEM((NZ, PAIR, D), BF16),
            pltpu.VMEM((2, 1, FW), F32),
            pltpu.VMEM((1, D), BF16),
            pltpu.VMEM((ROWS, D), BF16),
            pltpu.VMEM((8, CHIPS), jnp.int32),
            pltpu.VMEM((NZ, TOK, PAIR), BF16),
            pltpu.VMEM((TOK, PAIR), F32),
            pltpu.VMEM((TOK, D), F32),
            pltpu.VMEM((NX, NY, ROWS, D), BF16),
            pltpu.VMEM((2, 3, 4, ROWS, HD), BF16),
            pltpu.VMEM((2, 3, ROWS, HD), BF16),
            pltpu.VMEM((2, 3, ROWS, HD), BF16),
            pltpu.VMEM((ROWS, D), F32),
            pltpu.VMEM((NZ, 2, TOK, FW), BF16),
            pltpu.VMEM((NZ, FW, 2 * TOK), BF16),
            pltpu.VMEM((D, 2 * TOK), BF16),
            pltpu.VMEM((2, 2, TOK, FW), BF16),
            pltpu.VMEM((2, 4, 2, HALF, PAIR), BF16),
            pltpu.VMEM((2, 4, 2, HALF, PAIR), BF16),
            dma((NZ + 1,)), dma((NZ + 2,)), dma((NZ + 2,)),
            dma((2, 2, 3)), dma((2, 2, 3)),
            dma((2, 4, 2)), dma((2, 4, 2)),
            dma((2, 2, 3)), dma((2, 2, 3)),
            dma((2, 2, 3)), dma((2, 2, 3)),
            dma((2, 4, 2)), dma((2, 4, 2)),
            dma((4,)), dma((4,)),
            dma((5,)),
        ],
        compiler_params=pltpu.CompilerParams(
            collective_id=0, has_side_effects=True, vmem_limit_bytes=44 * 2**20
        ),
    )(x, we, be, wd, bd, tg, act)


def store_kernel(e_ref, b_ref, d_ref, eo_ref, bo_ref, do_ref, sem):
    copies = [pltpu.make_async_copy(e_ref, eo_ref, sem.at[0]), pltpu.make_async_copy(b_ref, bo_ref, sem.at[1])]
    copies += [pltpu.make_async_copy(d_ref.at[l], do_ref.at[l], sem.at[2 + l]) for l in range(NZ)]
    for cp in copies:
        cp.start()
    for cp in copies:
        cp.wait()


def store(e, b, d):
    hbm = pl.BlockSpec(memory_space=pl.ANY)
    return pl.pallas_call(
        store_kernel,
        name="store",
        out_shape=tuple(jax.ShapeDtypeStruct(a.shape, a.dtype) for a in (e, b, d)),
        in_specs=[hbm] * 3,
        out_specs=(hbm,) * 3,
        scratch_shapes=[pltpu.SemaphoreType.DMA((2 + NZ,))],
        compiler_params=pltpu.CompilerParams(vmem_limit_bytes=2**20),
    )(e, b, d)


def body(inputs, enc_weight, enc_bias, dec_weight, dec_bias, target, active):
    args = (inputs[0], enc_weight[0], enc_bias, dec_weight[0], dec_bias, target[0], active[0].T)
    enc_grad, bias_grad, dec_grad = fused(*(pltpu.with_memory_space_constraint(a, pltpu.HBM) for a in args))
    enc_grad, bias_grad, dec_grad = store(enc_grad, bias_grad, dec_grad)
    return enc_grad[None], bias_grad, dec_grad[None]


def solution(mesh):
    return jax.shard_map(
        body,
        mesh=mesh,
        in_specs=(
            P("section", "feat", None),
            P("section", None, "feat"),
            P("section", "feat"),
            P("section", None, "feat", None),
            P("section", None),
            P("section", "feat", None),
            P("section", None, None),
        ),
        out_specs=(
            P("section", None, "feat"),
            P("section", "feat"),
            P("section", None, "feat", None),
        ),
        check_vma=False,
    )
```

time: 110 us -> 88.7 us (0.81)
  Pallas kernels: 98.6 us -> 88 us
  matrix products: 8.29 us -> 0 us
  local copies, waits for them, and re-layouts: 1.37 us -> 0 us
    pallas_call x1 -> x2, Pallas kernels: 98.6 us -> 88 us  [the longest x1 85.4 us: fused(): pl.pallas_call(step_kernel, name='step', out_shape=(pltpu.VMEM((D, FW), B...]
    dot_general x2 -> x0, matrix products: 8.29 us -> none  [the longest x1 4.66 us: body(): jnp.einsum('ltf,td->lfd', codes, ra, preferred_element_type=F32)]
    squeeze x1 -> x0, local copies, waits for them, and re-layouts: 1.36 us -> none  [body(): active[0]]
where the time goes in v2:
time: 88.7 us; the launch traced here: 88.6 us
  Pallas kernels  88 us (99%)
    pallas_call x1, Pallas kernels, fused(): pl.pallas_call(step_kernel, name='step', out_shape=(pltpu.VMEM((D, FW), B...  85.4 us
    pallas_call x1, Pallas kernels, store(): pl.pallas_call(store_kernel, name='store', out_shape=tuple((jax.ShapeDtyp...  2.64 us

profile of v2, /device:TPU:1, one launch (start us, length us, event | category | flops | bytes accessed | tf_op | source)
XLA Modules:
  0.0 88.6 jit_solution(2158550968842666622)
XLA Ops:
  0.6 85.4 %step.1 = (bf16[2560,128]{1,0:T(8,128)(2,1)S(1)}, f32[1,128]{1,0:T(1,128)S(1)}, bf16[8,128,2560]{2,1,0:T(8,128)(2,1)S(1)}) custom-call(bf16[16,2560]{1,0:T(8,128)(2,1)} %bitcast.11, bf16[2560,128]{1,0:T(8,128)(2,1)} %bitcast.10, f32[1,128]{1,0:T(1,128)} %be_ref.1, bf16[8,128,2560]{2,1,0:T(8,128)(2,1)} %bitcast.9, bf16[1,2560]{1,0:T(2,128)(2,1)} %bd_ref.1, ...), custom_call_target="tpu_custom_call" | custom-call | tf_op jit(solution)/shard_map/step/pallas_call | solution.py:329
  86.0 2.6 %store.1 = (bf16[2560,128]{1,0:T(8,128)(2,1)}, f32[1,128]{1,0:T(1,128)}, bf16[8,128,2560]{2,1,0:T(8,128)(2,1)}) custom-call(bf16[2560,128]{1,0:T(8,128)(2,1)S(1)} %get-tuple-element.9.e_ref, f32[1,128]{1,0:T(1,128)S(1)} %get-tuple-element.10.b_ref, bf16[8,128,2560]{2,1,0:T(8,128)(2,1)S(1)} %get-tuple-element.11.d_ref), custom_call_target="tpu_custom_call" | custom-call | tf_op jit(solution)/shard_map/store/pallas_call | solution.py:388

commit v3 on v2

v3 whole, which is shorter than its diff:
```python
import functools

import jax
import jax.numpy as jnp
from jax import lax
from jax.experimental import pallas as pl
from jax.experimental.pallas import tpu as pltpu
from jax.sharding import PartitionSpec as P

MESH = pl.DeviceIdType.MESH
BF16 = jnp.bfloat16
F32 = jnp.float32

NX = 4
NY = 4
CHIPS = NX * NY
NZ = 8
ROWS = 16
FW = 128
D = 2560
TOK = CHIPS * ROWS
PAIR = 2 * FW
CUTS = 4
PIECE = TOK // CUTS
TILE = 512

HD = D // 2
QW = HD // 2
PARTS = [(axis, q) for q in (0, 1) for axis in (0, 1)]


def step_kernel(
    x_ref, we_ref, be_ref, wd_ref, bd_ref, tg_ref, act_ref,
    eg_ref, bg_ref, dg_ref,
    xg, rg, we_s, wd_s, be_s, bd_s, tg_s, act_s, vis, live, acc, rb, r1, r2s, r2, lhs, tot, cs, ct, xt, pg_s, zsb, zrb,
    in_sem, in_ssem, in_rsem, a_ssem, a_rsem, b_ssem, b_rsem, c_ssem, c_rsem,
    e_ssem, e_rsem, g_ssem, g_rsem, p_ssem, p_rsem, small_sem,
):
    s = lax.axis_index("section")
    f = lax.axis_index("feat")
    core = lax.rem(f, 2)
    chip = lax.div(f, 2)
    cx = lax.div(chip, NY)
    cy = lax.rem(chip, NY)

    def along(axis, step):
        x = lax.rem(cx + step, NX) if axis == 0 else cx
        y = lax.rem(cy + step, NY) if axis == 1 else cy
        return {"section": s, "feat": (x * NY + y) * 2 + core}

    peer = {"section": s, "feat": chip * 2 + 1 - core}
    up = {"section": lax.rem(s + 1, NZ), "feat": f}
    down = {"section": lax.rem(s + NZ - 1, NZ), "feat": f}
    up2 = {"section": lax.rem(s + 2, NZ), "feat": f}
    down2 = {"section": lax.rem(s + NZ - 2, NZ), "feat": f}

    def remote(src, dst, ssem, rsem, dev):
        return pltpu.make_async_remote_copy(
            src_ref=src, dst_ref=dst, send_sem=ssem, recv_sem=rsem, device_id=dev, device_id_type=MESH
        )

    barrier = pltpu.get_barrier_semaphore()
    for dev in [peer, up, down, up2, down2] + [along(axis, o) for axis in (0, 1) for o in (1, 2, 3)]:
        pl.semaphore_signal(barrier, inc=1, device_id=dev, device_id_type=MESH)

    loc = [pltpu.make_async_copy(we_ref, we_s.at[:, pl.ds(0, FW)], in_sem.at[NZ])]
    for l in range(NZ):
        loc.append(pltpu.make_async_copy(wd_ref.at[l], wd_s.at[l, pl.ds(0, FW)], in_sem.at[l]))
    small = [
        pltpu.make_async_copy(a, b, small_sem.at[k])
        for k, (a, b) in enumerate(
            [(act_ref, act_s), (be_ref, be_s.at[0]), (x_ref, xg.at[0, 0, 0]), (bd_ref, bd_s), (tg_ref, tg_s)]
        )
    ]
    for cp in small + loc:
        cp.start()

    pl.semaphore_wait(barrier, 11)

    def columns(axis, q):
        return pl.ds(axis * HD + q * QW, QW)

    def gather_first(axis, q, src, g, ssem, rsem):
        copies = {}
        for turn, way in ((0, axis), (1, 1 - axis)):
            for o in (2, 1, 3):
                there = (NX - o, 0) if way == 0 else (0, NY - o)
                cols = columns(axis, q)
                cp = remote(
                    src.at[:, cols], g.at[0, there[0], there[1], :, cols],
                    ssem.at[turn, q, axis, o - 1], rsem.at[turn, q, axis, o - 1], along(way, o),
                )
                cp.start()
                copies[turn, o] = cp
        return copies

    def gather_second(axis, q, first, g, ssem, rsem):
        copies = []
        for o in (1, 3, 2):
            first[0, o].wait_recv()
        for o in (2, 1, 3):
            cols = columns(axis, q)
            if axis == 0:
                src, dst = g.at[0, pl.ds(1, 3), 0, :, cols], g.at[0, pl.ds(1, 3), NY - o, :, cols]
            else:
                src, dst = g.at[0, 0, pl.ds(1, 3), :, cols], g.at[0, NX - o, pl.ds(1, 3), :, cols]
            cp = remote(src, dst, ssem.at[2, q, axis, o - 1], rsem.at[2, q, axis, o - 1], along(1 - axis, o))
            cp.start()
            copies.append(cp)
        return copies

    def gather_end(q, first, second):
        for axis in (0, 1):
            for o in (1, 3, 2):
                first[axis, q][1, o].wait_recv()
            for cp in second[axis, q]:
                cp.wait_recv()

    ag_x1 = {p: gather_first(*p, x_ref, xg, a_ssem, a_rsem) for p in PARTS}
    swap = [
        remote(we_ref, we_s.at[:, pl.ds(FW, FW)], in_ssem.at[NZ], in_rsem.at[NZ], peer),
        remote(be_ref, be_s.at[1], in_ssem.at[NZ + 1], in_rsem.at[NZ + 1], peer),
    ]
    for l in range(NZ):
        swap.append(remote(wd_ref.at[l], wd_s.at[l, pl.ds(FW, FW)], in_ssem.at[l], in_rsem.at[l], peer))
    for cp in swap:
        cp.start()

    small[0].wait()
    act = act_s[...]
    row_at = lax.broadcasted_iota(jnp.int32, (TOK, CHIPS), 0) // ROWS
    row_chip = lax.rem(cx + row_at // NY, NX) * NY + lax.rem(cy + lax.rem(row_at, NY), NY)
    expand = (row_chip == lax.broadcasted_iota(jnp.int32, (TOK, CHIPS), 1)).astype(F32)

    def keep_of(block):
        hit = jnp.max((act == block).astype(F32), axis=0, keepdims=True)
        return jnp.broadcast_to(jnp.sum(expand * hit, axis=1, keepdims=True), (TOK, FW))

    live[:, 0:FW] = keep_of(f)
    live[:, FW:PAIR] = keep_of(chip * 2 + 1 - core)

    ag_x = {p: gather_second(*p, ag_x1[p], xg, a_ssem, a_rsem) for p in PARTS}
    small[1].wait()
    small[2].wait()
    loc[0].wait()
    swap[0].wait_recv()
    swap[1].wait_recv()
    def pre_part(q, first, last):
        total = None
        for axis in (0, 1):
            at = axis * HD + q * QW
            x = xg[0, first:last, :, :, at:at + QW].reshape((last - first) * NY * ROWS, QW)
            part = jnp.dot(x, we_s[at:at + QW, :], preferred_element_type=F32)
            total = part if total is None else total + part
        return total

    def zcopy(way, hop, piece):
        held = 2 if hop == 4 else hop - 1
        block = lax.rem(s - held + NZ, NZ) if way == 0 else lax.rem(s + held, NZ)
        ref = vis.at[block, pl.ds(piece * PIECE, PIECE)]
        dev = ((up, up2), (down, down2))[way][hop == 4]
        return remote(ref, ref, b_ssem.at[way, hop - 1, piece], b_rsem.at[way, hop - 1, piece], dev)

    zsends = {}
    gather_end(0, ag_x1, ag_x)
    acc[:, 0:PAIR] = pre_part(0, 0, NX)
    bias = jnp.concatenate([be_s[0], be_s[1]], axis=1)
    gather_end(1, ag_x1, ag_x)
    for half in (0, 1):
        rows = slice(half * TOK // 2, (half + 1) * TOK // 2)
        pre = acc[rows, 0:PAIR] + pre_part(1, half * NX // 2, (half + 1) * NX // 2) + bias
        mask = live[rows, :] * (pre > 0).astype(F32)
        live[rows, :] = mask
        vis[s, rows, :] = (mask * pre).astype(BF16)
        for piece in range(half * CUTS // 2, (half + 1) * CUTS // 2):
            for way in (0, 1):
                cp = zcopy(way, 1, piece)
                cp.start()
                zsends[way, 1, piece] = cp

    swap_x = remote(xg.at[0], xg.at[1], p_ssem.at[0], p_rsem.at[0], peer)
    swap_x.start()

    for l in range(NZ):
        loc[1 + l].wait()
        swap[2 + l].wait_recv()

    def add_block(block, first=False):
        @pl.loop(0, D // TILE)
        def _(j):
            col = pl.ds(pl.multiple_of(j * TILE, TILE), TILE)
            part = jnp.dot(vis[block], wd_s[block, :, col], preferred_element_type=F32)
            if first:
                acc[:, col] = part
            else:
                acc[:, col] += part

    add_block(s, True)
    for hop in (1, 2, 3):
        for piece in range(CUTS):
            for way in (0, 1):
                zsends[way, hop, piece].wait_recv()
                for later in ((2,), (3, 4) if piece * 2 // CUTS == way else (3,), ())[hop - 1]:
                    cp = zcopy(way, later, piece)
                    cp.start()
                    zsends[way, later, piece] = cp

        if hop < 3:

            @pl.when(s >= hop)
            def _():
                add_block(lax.rem(s - hop + NZ, NZ))

            @pl.when(s + hop >= NZ)
            def _():
                add_block(lax.rem(s + hop, NZ))

    for way in (0, 1):
        for piece in range(way * CUTS // 2, (way + 1) * CUTS // 2):
            zsends[way, 4, piece].wait_recv()
    last = [(lax.rem(s + NZ - 3, NZ), s >= 3), (lax.rem(s + 3, NZ), s + 3 >= NZ), (lax.rem(s + 4, NZ), s >= 4)]
    for k, (block, given) in enumerate(last):
        codes = vis[block]
        lhs[:, k * PAIR:(k + 1) * PAIR] = jnp.where(given, codes, jnp.zeros_like(codes))

    rs1 = {}
    for axis, q in PARTS:
        at = axis * HD + q * QW
        cols = slice(at, at + QW)
        rhs = jnp.concatenate([wd_s[block, :, cols] for block, _ in last], axis=0)
        part = acc[:, cols] + jnp.dot(lhs[...], rhs, preferred_element_type=F32)
        acc[:, cols] = part
        rb[:, :, :, cols] = part.astype(BF16).reshape(NX, NY, ROWS, QW)
        for o in (2, 1, 3):
            src = rb.at[o, :, :, columns(axis, q)] if axis == 0 else rb.at[:, o, :, columns(axis, q)]
            cp = remote(
                src, r1.at[axis, q, o - 1], c_ssem.at[0, q, axis, o - 1], c_rsem.at[0, q, axis, o - 1], along(axis, o)
            )
            cp.start()
            rs1[axis, q, o] = cp
    swap_c = remote(vis.at[:, :, pl.ds(FW, FW)], cs.at[:, 1], p_ssem.at[1], p_rsem.at[1], peer)
    swap_c.start()
    cs[:, 0] = vis[:, :, 0:FW]
    xt[:, 0:TOK] = xg[0].reshape(TOK, D).T
    small[3].wait()
    small[4].wait()
    rs2 = {}
    for axis, q in PARTS:
        at = axis * HD + q * QW
        cols = slice(at, at + QW)
        for o in (1, 3, 2):
            rs1[axis, q, o].wait_recv()
        for o in (2, 1, 3, 0):
            row = (o if axis == 0 else o * NY) * ROWS
            part = acc[row:row + ROWS, cols]
            for k in range(3):
                part = part + r1[axis, q, k, o].astype(F32)
            if o == 0:
                tot[:, cols] = part + bd_s[:, cols].astype(F32) - tg_s[:, cols].astype(F32)
            else:
                r2s[axis, q, o - 1] = part.astype(BF16)
                cp = remote(
                    r2s.at[axis, q, o - 1], r2.at[axis, q, o - 1],
                    c_ssem.at[1, q, axis, o - 1], c_rsem.at[1, q, axis, o - 1], along(1 - axis, o),
                )
                cp.start()
                rs2[axis, q, o] = cp

    ag_r1 = {}
    for axis, q in PARTS:
        at = axis * HD + q * QW
        cols = slice(at, at + QW)
        part = tot[:, cols]
        for o in (1, 3, 2):
            rs2[axis, q, o].wait_recv()
            part = part + r2[axis, q, o - 1].astype(F32)
        rg[0, 0, 0, :, cols] = part.astype(BF16)
        ag_r1[axis, q] = gather_first(axis, q, rg.at[0, 0, 0], rg, e_ssem, e_rsem)
    ag_r = {p: gather_second(*p, ag_r1[p], rg, e_ssem, e_rsem) for p in PARTS}
    swap_x.wait_recv()
    xt[:, TOK:2 * TOK] = xg[1].reshape(TOK, D).T
    swap_c.wait_recv()
    for l in range(NZ):
        seen = cs[l].reshape(2 * TOK, FW).T
        ct[l] = jnp.where(s >= l, seen, jnp.zeros_like(seen))
    def grad_cols(block, at, width):
        return lax.dot_general(
            rg[0, :, :, :, at:at + width].reshape(TOK, width), wd_s[block, :, at:at + width],
            (((1,), (1,)), ((), ())), preferred_element_type=F32,
        )

    def grad_part(block, q):
        return grad_cols(block, q * QW, QW) + grad_cols(block, HD + q * QW, QW)

    def far(way, j):
        if way == 0:
            return lax.rem(s - j + NZ, NZ), s >= j
        return lax.rem(s + j, NZ), s + j >= NZ

    def gcopy(way, j, piece):
        return remote(
            zsb.at[way, j - 1, piece], zrb.at[way, j - 1, piece],
            g_ssem.at[way, j - 1, piece], g_rsem.at[way, j - 1, piece], ((down, down2), (up, up2))[way][j == 4],
        )

    gsends = {}

    def pass_on(way, j, piece, slot, given):
        part = jnp.where(given, acc[piece * PIECE:(piece + 1) * PIECE, slot * PAIR:(slot + 1) * PAIR], 0.0)
        for k in {2: (4, 3) if piece * 2 // CUTS == way else (3,), 1: (2,)}.get(j, ()):
            gsends[way, k, piece].wait_recv()
            part = part + zrb[way, k - 1, piece].astype(F32)
        zsb[way, j - 1, piece] = part.astype(BF16)
        cp = gcopy(way, j, piece)
        cp.start()
        gsends[way, j, piece] = cp

    gather_end(0, ag_r1, ag_r)
    for way in (0, 1):
        acc[:, way * PAIR:(way + 1) * PAIR] = grad_part(far(way, 3)[0], 0)
    gather_end(1, ag_r1, ag_r)
    for way in (0, 1):
        acc[:, way * PAIR:(way + 1) * PAIR] += grad_part(far(way, 3)[0], 1)
        for piece in range(CUTS):
            pass_on(way, 3, piece, way, far(way, 3)[1])
    acc[:, 0:PAIR] = grad_cols(far(0, 4)[0], 0, D)
    for piece in range(CUTS):
        pass_on(piece * 2 // CUTS, 4, piece, 0, far(0, 4)[1])
    swap_r = remote(rg.at[0], rg.at[1], p_ssem.at[2], p_rsem.at[2], peer)
    swap_r.start()

    def dec_tile(j):
        col = slice(j * TILE, (j + 1) * TILE)
        part = jnp.dot(
            ct[...].reshape(NZ * FW, 2 * TOK), rg[...].reshape(2 * TOK, D)[:, col], preferred_element_type=F32
        )
        dg_ref[:, :, col] = part.astype(BF16).reshape(NZ, FW, TILE)

    for j in (2, 1):
        for way in (0, 1):
            acc[:, way * PAIR:(way + 1) * PAIR] = grad_cols(far(way, j)[0], 0, D)
        if j == 1:
            swap_r.wait_recv()
            dec_tile(0)
        for piece in range(CUTS):
            for way in (0, 1):
                pass_on(way, j, piece, way, far(way, j)[1])

    acc[:, 0:PAIR] = grad_cols(s, 0, D)
    for j in range(1, D // TILE):
        dec_tile(j)
    for piece in range(CUTS):
        rows = slice(piece * PIECE, (piece + 1) * PIECE)
        own = acc[rows, 0:PAIR]
        for way in (0, 1):
            gsends[way, 1, piece].wait_recv()
            own = own + zrb[way, 0, piece].astype(F32)
        grad = (own * live[rows, :]).astype(BF16)
        pg_s[0, 0, rows, :] = grad[:, 0:FW]
        pg_s[1, 0, rows, :] = grad[:, FW:PAIR]
    swap_g = remote(pg_s.at[1, 0], pg_s.at[0, 1], p_ssem.at[3], p_rsem.at[3], peer)
    swap_g.start()
    own = jnp.dot(xt[:, 0:TOK], pg_s[0, 0], preferred_element_type=F32)
    swap_g.wait_recv()
    eg_ref[...] = (own + jnp.dot(xt[:, TOK:2 * TOK], pg_s[0, 1], preferred_element_type=F32)).astype(BF16)
    bg_ref[...] = jnp.sum(pg_s[0].reshape(2 * TOK, FW).astype(F32), axis=0, keepdims=True)

    for first in list(ag_x1.values()) + list(ag_r1.values()):
        for cp in first.values():
            cp.wait_send()
    for cp in list(rs1.values()) + list(rs2.values()):
        cp.wait_send()
    for copies in list(ag_x.values()) + list(ag_r.values()):
        for cp in copies:
            cp.wait_send()
    for cp in swap + [swap_x, swap_c, swap_r, swap_g]:
        cp.wait_send()
    for cp in list(zsends.values()) + list(gsends.values()):
        cp.wait_send()


def fused(x, we, be, wd, bd, tg, act):
    vmem = pl.BlockSpec(memory_space=pltpu.VMEM)
    hbm = pl.BlockSpec(memory_space=pl.ANY)
    dma = pltpu.SemaphoreType.DMA
    return pl.pallas_call(
        step_kernel,
        name="step",
        out_shape=(
            pltpu.VMEM((D, FW), BF16),
            pltpu.VMEM((1, FW), F32),
            pltpu.VMEM((NZ, FW, D), BF16),
        ),
        in_specs=[pl.BlockSpec(memory_space=pltpu.HBM)] * 7,
        out_specs=(vmem, vmem, vmem),
        scratch_shapes=[
            pltpu.VMEM((2, NX, NY, ROWS, D), BF16),
            pltpu.VMEM((2, NX, NY, ROWS, D), BF16),
            pltpu.VMEM((D, PAIR), BF16),
            pltpu.VMEM((NZ, PAIR, D), BF16),
            pltpu.VMEM((2, 1, FW), F32),
            pltpu.VMEM((1, D), BF16),
            pltpu.VMEM((ROWS, D), BF16),
            pltpu.VMEM((8, CHIPS), jnp.int32),
            pltpu.VMEM((NZ, TOK, PAIR), BF16),
            pltpu.VMEM((TOK, PAIR), F32),
            pltpu.VMEM((TOK, D), F32),
            pltpu.VMEM((NX, NY, ROWS, D), BF16),
            pltpu.VMEM((2, 2, 3, 4, ROWS, QW), BF16),
            pltpu.VMEM((2, 2, 3, ROWS, QW), BF16),
            pltpu.VMEM((2, 2, 3, ROWS, QW), BF16),
            pltpu.VMEM((TOK, 3 * PAIR), BF16),
            pltpu.VMEM((ROWS, D), F32),
            pltpu.VMEM((NZ, 2, TOK, FW), BF16),
            pltpu.VMEM((NZ, FW, 2 * TOK), BF16),
            pltpu.VMEM((D, 2 * TOK), BF16),
            pltpu.VMEM((2, 2, TOK, FW), BF16),
            pltpu.VMEM((2, 4, CUTS, PIECE, PAIR), BF16),
            pltpu.VMEM((2, 4, CUTS, PIECE, PAIR), BF16),
            dma((NZ + 1,)), dma((NZ + 2,)), dma((NZ + 2,)),
            dma((3, 2, 2, 3)), dma((3, 2, 2, 3)),
            dma((2, 4, CUTS)), dma((2, 4, CUTS)),
            dma((3, 2, 2, 3)), dma((3, 2, 2, 3)),
            dma((3, 2, 2, 3)), dma((3, 2, 2, 3)),
            dma((2, 4, CUTS)), dma((2, 4, CUTS)),
            dma((4,)), dma((4,)),
            dma((5,)),
        ],
        compiler_params=pltpu.CompilerParams(
            collective_id=0, has_side_effects=True, vmem_limit_bytes=44 * 2**20
        ),
    )(x, we, be, wd, bd, tg, act)


def store_kernel(e_ref, b_ref, d_ref, eo_ref, bo_ref, do_ref, sem):
    copies = [pltpu.make_async_copy(e_ref, eo_ref, sem.at[0]), pltpu.make_async_copy(b_ref, bo_ref, sem.at[1])]
    copies += [pltpu.make_async_copy(d_ref.at[l], do_ref.at[l], sem.at[2 + l]) for l in range(NZ)]
    for cp in copies:
        cp.start()
    for cp in copies:
        cp.wait()


def store(e, b, d):
    hbm = pl.BlockSpec(memory_space=pl.ANY)
    return pl.pallas_call(
        store_kernel,
        name="store",
        out_shape=tuple(jax.ShapeDtypeStruct(a.shape, a.dtype) for a in (e, b, d)),
        in_specs=[hbm] * 3,
        out_specs=(hbm,) * 3,
        scratch_shapes=[pltpu.SemaphoreType.DMA((2 + NZ,))],
        compiler_params=pltpu.CompilerParams(vmem_limit_bytes=2**20),
    )(e, b, d)


def body(inputs, enc_weight, enc_bias, dec_weight, dec_bias, target, active):
    args = (inputs[0], enc_weight[0], enc_bias, dec_weight[0], dec_bias, target[0], active[0].T)
    enc_grad, bias_grad, dec_grad = fused(*(pltpu.with_memory_space_constraint(a, pltpu.HBM) for a in args))
    enc_grad, bias_grad, dec_grad = store(enc_grad, bias_grad, dec_grad)
    return enc_grad[None], bias_grad, dec_grad[None]


def solution(mesh):
    return jax.shard_map(
        body,
        mesh=mesh,
        in_specs=(
            P("section", "feat", None),
            P("section", None, "feat"),
            P("section", "feat"),
            P("section", None, "feat", None),
            P("section", None),
            P("section", "feat", None),
            P("section", None, None),
        ),
        out_specs=(
            P("section", None, "feat"),
            P("section", "feat"),
            P("section", None, "feat", None),
        ),
        check_vma=False,
    )
```

time: 88.7 us -> 81.7 us (0.921)
  Pallas kernels: 88 us -> 81 us
    pallas_call x1, Pallas kernels: 85.4 us -> 78.3 us  [fused(): pl.pallas_call(step_kernel, name='step', out_shape=(pltpu.VMEM((D, FW), B...]
where the time goes in v3:
time: 81.7 us; the launch traced here: 81.6 us
  Pallas kernels  81 us (99%)
    pallas_call x1, Pallas kernels, fused(): pl.pallas_call(step_kernel, name='step', out_shape=(pltpu.VMEM((D, FW), B...  78.3 us
    pallas_call x1, Pallas kernels, store(): pl.pallas_call(store_kernel, name='store', out_shape=tuple((jax.ShapeDtyp...  2.64 us

profile of v3, /device:TPU:1, one launch (start us, length us, event | category | flops | bytes accessed | tf_op | source)
XLA Modules:
  0.0 81.6 jit_solution(5415592036243179168)
XLA Ops:
  0.6 78.3 %step.1 = (bf16[2560,128]{1,0:T(8,128)(2,1)S(1)}, f32[1,128]{1,0:T(1,128)S(1)}, bf16[8,128,2560]{2,1,0:T(8,128)(2,1)S(1)}) custom-call(bf16[16,2560]{1,0:T(8,128)(2,1)} %bitcast.11, bf16[2560,128]{1,0:T(8,128)(2,1)} %bitcast.10, f32[1,128]{1,0:T(1,128)} %be_ref.1, bf16[8,128,2560]{2,1,0:T(8,128)(2,1)} %bitcast.9, bf16[1,2560]{1,0:T(2,128)(2,1)} %bd_ref.1, ...), custom_call_target="tpu_custom_call" | custom-call | tf_op jit(solution)/shard_map/step/pallas_call | solution.py:386
  79.0 2.6 %store.1 = (bf16[2560,128]{1,0:T(8,128)(2,1)}, f32[1,128]{1,0:T(1,128)}, bf16[8,128,2560]{2,1,0:T(8,128)(2,1)}) custom-call(bf16[2560,128]{1,0:T(8,128)(2,1)S(1)} %get-tuple-element.9.e_ref, f32[1,128]{1,0:T(1,128)S(1)} %get-tuple-element.10.b_ref, bf16[8,128,2560]{2,1,0:T(8,128)(2,1)S(1)} %get-tuple-element.11.d_ref), custom_call_target="tpu_custom_call" | custom-call | tf_op jit(solution)/shard_map/store/pallas_call | solution.py:446

commit v4 on v3

--- a/solution.py
+++ b/solution.py
@@ -33,7 +33,7 @@
     x_ref, we_ref, be_ref, wd_ref, bd_ref, tg_ref, act_ref,
     eg_ref, bg_ref, dg_ref,
     xg, rg, we_s, wd_s, be_s, bd_s, tg_s, act_s, vis, live, acc, rb, r1, r2s, r2, lhs, tot, cs, ct, xt, pg_s, zsb, zrb,
-    in_sem, in_ssem, in_rsem, a_ssem, a_rsem, b_ssem, b_rsem, c_ssem, c_rsem,
+    in_sem, in_ssem, in_rsem, a_ssem, a_rsem, a2_ssem, a2_rsem, b_ssem, b_rsem, c_ssem, c_rsem,
     e_ssem, e_rsem, g_ssem, g_rsem, p_ssem, p_rsem, small_sem,
 ):
     s = lax.axis_index("section")
@@ -80,9 +80,10 @@
     def columns(axis, q):
         return pl.ds(axis * HD + q * QW, QW)
 
-    def gather_first(axis, q, src, g, ssem, rsem):
-        copies = {}
-        for turn, way in ((0, axis), (1, 1 - axis)):
+    def gather_first(axis, q, src, g, ssem, rsem, turns=(0, 1), copies=None):
+        copies = {} if copies is None else copies
+        for turn in turns:
+            way = axis if turn == 0 else 1 - axis
             for o in (2, 1, 3):
                 there = (NX - o, 0) if way == 0 else (0, NY - o)
                 cols = columns(axis, q)
@@ -94,7 +95,40 @@
                 copies[turn, o] = cp
         return copies
 
-    def gather_second(axis, q, first, g, ssem, rsem):
+    def gather_second(half, first, g, ssem, rsem):
+        copies = {}
+        for axis, q in [(a, b) for b in (0, 1) for a in (0, 1)]:
+            cols = columns(axis, q)
+            if axis == 0:
+                for o in ((3,), (1, 2))[half]:
+                    first[axis, q][0, o].wait_recv()
+                at, count = ((1, 1), (2, 2))[half]
+                for o in (2, 1, 3):
+                    src, dst = g.at[0, pl.ds(at, count), 0, :, cols], g.at[0, pl.ds(at, count), NY - o, :, cols]
+                    k = half * 3 + o - 1
+                    copies[axis, q, o] = remote(src, dst, ssem.at[q, axis, k], rsem.at[q, axis, k], along(1, o))
+                    copies[axis, q, o].start()
+            else:
+                if half == 0:
+                    for o in (1, 3, 2):
+                        first[axis, q][0, o].wait_recv()
+                for o in ((3,), (2, 1))[half]:
+                    src, dst = g.at[0, 0, pl.ds(1, 3), :, cols], g.at[0, NX - o, pl.ds(1, 3), :, cols]
+                    copies[axis, q, o] = remote(src, dst, ssem.at[q, axis, o - 1], rsem.at[q, axis, o - 1], along(0, o))
+                    copies[axis, q, o].start()
+        return copies
+
+    def gather_end(half, first, second):
+        for q in (0, 1):
+            if half == 0:
+                for o in (1, 3, 2):
+                    first[0, q][1, o].wait_recv()
+            for o in ((3,), (1, 2))[half]:
+                first[1, q][1, o].wait_recv()
+        for cp in second[half].values():
+            cp.wait_recv()
+
+    def gather_second_q(axis, q, first, g, ssem, rsem):
         copies = []
         for o in (1, 3, 2):
             first[0, o].wait_recv()
@@ -109,14 +143,16 @@
             copies.append(cp)
         return copies
 
-    def gather_end(q, first, second):
+    def gather_end_q(q, first, second):
         for axis in (0, 1):
             for o in (1, 3, 2):
                 first[axis, q][1, o].wait_recv()
             for cp in second[axis, q]:
                 cp.wait_recv()
 
-    ag_x1 = {p: gather_first(*p, x_ref, xg, a_ssem, a_rsem) for p in PARTS}
+    ag_x1 = {p: gather_first(*p, x_ref, xg, a_ssem, a_rsem, (0,)) for p in PARTS}
+    for p in PARTS:
+        gather_first(*p, x_ref, xg, a_ssem, a_rsem, (1,), ag_x1[p])
     swap = [
         remote(we_ref, we_s.at[:, pl.ds(FW, FW)], in_ssem.at[NZ], in_rsem.at[NZ], peer),
         remote(be_ref, be_s.at[1], in_ssem.at[NZ + 1], in_rsem.at[NZ + 1], peer),
@@ -139,21 +175,12 @@
     live[:, 0:FW] = keep_of(f)
     live[:, FW:PAIR] = keep_of(chip * 2 + 1 - core)
 
-    ag_x = {p: gather_second(*p, ag_x1[p], xg, a_ssem, a_rsem) for p in PARTS}
+    ag_x = [gather_second(half, ag_x1, xg, a2_ssem, a2_rsem) for half in (0, 1)]
     small[1].wait()
     small[2].wait()
     loc[0].wait()
     swap[0].wait_recv()
     swap[1].wait_recv()
-    def pre_part(q, first, last):
-        total = None
-        for axis in (0, 1):
-            at = axis * HD + q * QW
-            x = xg[0, first:last, :, :, at:at + QW].reshape((last - first) * NY * ROWS, QW)
-            part = jnp.dot(x, we_s[at:at + QW, :], preferred_element_type=F32)
-            total = part if total is None else total + part
-        return total
-
     def zcopy(way, hop, piece):
         held = 2 if hop == 4 else hop - 1
         block = lax.rem(s - held + NZ, NZ) if way == 0 else lax.rem(s + held, NZ)
@@ -162,13 +189,12 @@
         return remote(ref, ref, b_ssem.at[way, hop - 1, piece], b_rsem.at[way, hop - 1, piece], dev)
 
     zsends = {}
-    gather_end(0, ag_x1, ag_x)
-    acc[:, 0:PAIR] = pre_part(0, 0, NX)
     bias = jnp.concatenate([be_s[0], be_s[1]], axis=1)
-    gather_end(1, ag_x1, ag_x)
     for half in (0, 1):
+        gather_end(half, ag_x1, ag_x)
         rows = slice(half * TOK // 2, (half + 1) * TOK // 2)
-        pre = acc[rows, 0:PAIR] + pre_part(1, half * NX // 2, (half + 1) * NX // 2) + bias
+        x = xg[0, half * NX // 2:(half + 1) * NX // 2].reshape(TOK // 2, D)
+        pre = jnp.dot(x, we_s[...], preferred_element_type=F32) + bias
         mask = live[rows, :] * (pre > 0).astype(F32)
         live[rows, :] = mask
         vis[s, rows, :] = (mask * pre).astype(BF16)
@@ -200,7 +226,7 @@
         for piece in range(CUTS):
             for way in (0, 1):
                 zsends[way, hop, piece].wait_recv()
-                for later in ((2,), (3, 4) if piece * 2 // CUTS == way else (3,), ())[hop - 1]:
+                for later in ((2,), (4, 3) if piece * 2 // CUTS == way else (3,), ())[hop - 1]:
                     cp = zcopy(way, later, piece)
                     cp.start()
                     zsends[way, later, piece] = cp
@@ -275,8 +301,11 @@
             rs2[axis, q, o].wait_recv()
             part = part + r2[axis, q, o - 1].astype(F32)
         rg[0, 0, 0, :, cols] = part.astype(BF16)
-        ag_r1[axis, q] = gather_first(axis, q, rg.at[0, 0, 0], rg, e_ssem, e_rsem)
-    ag_r = {p: gather_second(*p, ag_r1[p], rg, e_ssem, e_rsem) for p in PARTS}
+        ag_r1[axis, q] = gather_first(axis, q, rg.at[0, 0, 0], rg, e_ssem, e_rsem, (0,))
+        if axis == 1:
+            for a in (0, 1):
+                gather_first(a, q, rg.at[0, 0, 0], rg, e_ssem, e_rsem, (1,), ag_r1[a, q])
+    ag_r = {p: gather_second_q(*p, ag_r1[p], rg, e_ssem, e_rsem) for p in PARTS}
     swap_x.wait_recv()
     xt[:, TOK:2 * TOK] = xg[1].reshape(TOK, D).T
     swap_c.wait_recv()
@@ -315,10 +344,10 @@
         cp.start()
         gsends[way, j, piece] = cp
 
-    gather_end(0, ag_r1, ag_r)
+    gather_end_q(0, ag_r1, ag_r)
     for way in (0, 1):
         acc[:, way * PAIR:(way + 1) * PAIR] = grad_part(far(way, 3)[0], 0)
-    gather_end(1, ag_r1, ag_r)
+    gather_end_q(1, ag_r1, ag_r)
     for way in (0, 1):
         acc[:, way * PAIR:(way + 1) * PAIR] += grad_part(far(way, 3)[0], 1)
         for piece in range(CUTS):
@@ -370,7 +399,10 @@
             cp.wait_send()
     for cp in list(rs1.values()) + list(rs2.values()):
         cp.wait_send()
-    for copies in list(ag_x.values()) + list(ag_r.values()):
+    for copies in ag_x:
+        for cp in copies.values():
+            cp.wait_send()
+    for copies in ag_r.values():
         for cp in copies:
             cp.wait_send()
     for cp in swap + [swap_x, swap_c, swap_r, swap_g]:
@@ -418,9 +450,10 @@
             pltpu.VMEM((2, 4, CUTS, PIECE, PAIR), BF16),
             pltpu.VMEM((2, 4, CUTS, PIECE, PAIR), BF16),
             dma((NZ + 1,)), dma((NZ + 2,)), dma((NZ + 2,)),
-            dma((3, 2, 2, 3)), dma((3, 2, 2, 3)),
+            dma((2, 2, 2, 3)), dma((2, 2, 2, 3)),
+            dma((2, 2, 6)), dma((2, 2, 6)),
             dma((2, 4, CUTS)), dma((2, 4, CUTS)),
-            dma((3, 2, 2, 3)), dma((3, 2, 2, 3)),
+            dma((2, 2, 2, 3)), dma((2, 2, 2, 3)),
             dma((3, 2, 2, 3)), dma((3, 2, 2, 3)),
             dma((2, 4, CUTS)), dma((2, 4, CUTS)),
             dma((4,)), dma((4,)),

time: 81.7 us -> 79.9 us (0.978)
  Pallas kernels: 81 us -> 79.1 us
    pallas_call x1, Pallas kernels: 78.3 us -> 76.5 us  [fused(): pl.pallas_call(step_kernel, name='step', out_shape=(pltpu.VMEM((D, FW), B...]
where the time goes in v4:
time: 79.9 us; the launch traced here: 79.8 us
  Pallas kernels  79.1 us (99%)
    pallas_call x1, Pallas kernels, fused(): pl.pallas_call(step_kernel, name='step', out_shape=(pltpu.VMEM((D, FW), B...  76.5 us
    pallas_call x1, Pallas kernels, store(): pl.pallas_call(store_kernel, name='store', out_shape=tuple((jax.ShapeDtyp...  2.64 us

profile of v4, /device:TPU:1, one launch (start us, length us, event | category | flops | bytes accessed | tf_op | source)
XLA Modules:
  0.0 79.8 jit_solution(4697907599167021582)
XLA Ops:
  0.6 76.5 %step.1 = (bf16[2560,128]{1,0:T(8,128)(2,1)S(1)}, f32[1,128]{1,0:T(1,128)S(1)}, bf16[8,128,2560]{2,1,0:T(8,128)(2,1)S(1)}) custom-call(bf16[16,2560]{1,0:T(8,128)(2,1)} %bitcast.11, bf16[2560,128]{1,0:T(8,128)(2,1)} %bitcast.10, f32[1,128]{1,0:T(1,128)} %be_ref.1, bf16[8,128,2560]{2,1,0:T(8,128)(2,1)} %bitcast.9, bf16[1,2560]{1,0:T(2,128)(2,1)} %bd_ref.1, ...), custom_call_target="tpu_custom_call" | custom-call | tf_op jit(solution)/shard_map/step/pallas_call | solution.py:418
  77.1 2.6 %store.1 = (bf16[2560,128]{1,0:T(8,128)(2,1)}, f32[1,128]{1,0:T(1,128)}, bf16[8,128,2560]{2,1,0:T(8,128)(2,1)}) custom-call(bf16[2560,128]{1,0:T(8,128)(2,1)S(1)} %get-tuple-element.9.e_ref, f32[1,128]{1,0:T(1,128)S(1)} %get-tuple-element.10.b_ref, bf16[8,128,2560]{2,1,0:T(8,128)(2,1)S(1)} %get-tuple-element.11.d_ref), custom_call_target="tpu_custom_call" | custom-call | tf_op jit(solution)/shard_map/store/pallas_call | solution.py:479

commit v5 on v4

--- a/solution.py
+++ b/solution.py
@@ -378,6 +378,7 @@
     acc[:, 0:PAIR] = grad_cols(s, 0, D)
     for j in range(1, D // TILE):
         dec_tile(j)
+    swap_g = []
     for piece in range(CUTS):
         rows = slice(piece * PIECE, (piece + 1) * PIECE)
         own = acc[rows, 0:PAIR]
@@ -387,10 +388,14 @@
         grad = (own * live[rows, :]).astype(BF16)
         pg_s[0, 0, rows, :] = grad[:, 0:FW]
         pg_s[1, 0, rows, :] = grad[:, FW:PAIR]
-    swap_g = remote(pg_s.at[1, 0], pg_s.at[0, 1], p_ssem.at[3], p_rsem.at[3], peer)
-    swap_g.start()
+        if piece % 2 == 1:
+            part = pl.ds((piece - 1) * PIECE, 2 * PIECE)
+            k = 3 + piece // 2
+            swap_g.append(remote(pg_s.at[1, 0, part], pg_s.at[0, 1, part], p_ssem.at[k], p_rsem.at[k], peer))
+            swap_g[-1].start()
     own = jnp.dot(xt[:, 0:TOK], pg_s[0, 0], preferred_element_type=F32)
-    swap_g.wait_recv()
+    for cp in swap_g:
+        cp.wait_recv()
     eg_ref[...] = (own + jnp.dot(xt[:, TOK:2 * TOK], pg_s[0, 1], preferred_element_type=F32)).astype(BF16)
     bg_ref[...] = jnp.sum(pg_s[0].reshape(2 * TOK, FW).astype(F32), axis=0, keepdims=True)
 
@@ -405,7 +410,7 @@
     for copies in ag_r.values():
         for cp in copies:
             cp.wait_send()
-    for cp in swap + [swap_x, swap_c, swap_r, swap_g]:
+    for cp in swap + [swap_x, swap_c, swap_r] + swap_g:
         cp.wait_send()
     for cp in list(zsends.values()) + list(gsends.values()):
         cp.wait_send()
@@ -456,7 +461,7 @@
             dma((2, 2, 2, 3)), dma((2, 2, 2, 3)),
             dma((3, 2, 2, 3)), dma((3, 2, 2, 3)),
             dma((2, 4, CUTS)), dma((2, 4, CUTS)),
-            dma((4,)), dma((4,)),
+            dma((5,)), dma((5,)),
             dma((5,)),
         ],
         compiler_params=pltpu.CompilerParams(

time: 79.9 us -> 79.8 us (level)
  no operation moved by 1% of the time
where the time goes in v5:
time: 79.8 us
  Pallas kernels  79.1 us (99%)
    pallas_call x1, Pallas kernels, fused(): pl.pallas_call(step_kernel, name='step', out_shape=(pltpu.VMEM((D, FW), B...  76.5 us
    pallas_call x1, Pallas kernels, store(): pl.pallas_call(store_kernel, name='store', out_shape=tuple((jax.ShapeDtyp...  2.64 us

profile of v5, /device:TPU:1, one launch (start us, length us, event | category | flops | bytes accessed | tf_op | source)
XLA Modules:
  0.0 79.8 jit_solution(12166505377228890476)
XLA Ops:
  0.6 76.5 %step.1 = (bf16[2560,128]{1,0:T(8,128)(2,1)S(1)}, f32[1,128]{1,0:T(1,128)S(1)}, bf16[8,128,2560]{2,1,0:T(8,128)(2,1)S(1)}) custom-call(bf16[16,2560]{1,0:T(8,128)(2,1)} %bitcast.11, bf16[2560,128]{1,0:T(8,128)(2,1)} %bitcast.10, f32[1,128]{1,0:T(1,128)} %be_ref.1, bf16[8,128,2560]{2,1,0:T(8,128)(2,1)} %bitcast.9, bf16[1,2560]{1,0:T(2,128)(2,1)} %bd_ref.1, ...), custom_call_target="tpu_custom_call" | custom-call | tf_op jit(solution)/shard_map/step/pallas_call | solution.py:423
  77.1 2.6 %store.1 = (bf16[2560,128]{1,0:T(8,128)(2,1)}, f32[1,128]{1,0:T(1,128)}, bf16[8,128,2560]{2,1,0:T(8,128)(2,1)}) custom-call(bf16[2560,128]{1,0:T(8,128)(2,1)S(1)} %get-tuple-element.9.e_ref, f32[1,128]{1,0:T(1,128)S(1)} %get-tuple-element.10.b_ref, bf16[8,128,2560]{2,1,0:T(8,128)(2,1)S(1)} %get-tuple-element.11.d_ref), custom_call_target="tpu_custom_call" | custom-call | tf_op jit(solution)/shard_map/store/pallas_call | solution.py:484
